TPU v7x, 512 devices: a whole 4x4x16 slice. The times are simulated.
512 devices in a mesh: dp: 32 (over z, core), expert: 16 (over x, y).
Axes of the slice: x: 4, y: 4, z: 16, core: 2. Of those that a mesh axis runs over, the one named last changes fastest.
Arguments:
- cotangent: bfloat16 [196608, 1024], P(('dp', 'expert')), may hold values from -0.119628906 to 0.119628906
- route: int32 [196608, 1], P(('dp', 'expert')), may hold values from 0 to 15; in each aligned block of 384 rows (0 to 383, 384 to 767, ...) at most 72 rows name the same one
- hidden: bfloat16 [32, 16, 1152, 768], P('dp', 'expert'), may hold values from -6 to 6
- master: float32 [16, 768, 1024], P('expert', 'dp'), may hold values from -0.21875 to 0.21875
- moment_one: float32 [16, 768, 1024], P('expert', 'dp'), may hold values from -1.8 to 1.8
- moment_two: float32 [16, 768, 1024], P('expert', 'dp'), may hold values from 0.05 to 0.5
Outputs:
- master_next: float32 [16, 768, 1024], P('expert', 'dp')
- moment_one_next: float32 [16, 768, 1024], P('expert', 'dp')
- moment_two_next: float32 [16, 768, 1024], P('expert', 'dp')
- weights: bfloat16 [16, 768, 1024], P('expert')
Inputs may be any that keep to these rules, and one draw needn't show every extreme that they name: `route`: among the tokens of one device no expert is named more than 72 times, and on some device one expert is named exactly 72 times.
All inputs are finite; a program needn't handle non-finite values.
Results may differ from a plain program's by a relative error of at most 0.001.
Values may be sent and summed in bfloat16 or wider, within the bound.
No kernel may reach another device: no remote copies, remote signals or barrier semaphores. Data moves between devices by JAX's collectives and lax.ppermute only.
A program may use at most 64 MiB of HBM per device.

v0:
```python
import jax
import jax.numpy as jnp
from jax import lax
from jax.sharding import PartitionSpec as P

STEP = 10


def local(cotangent, route, hidden, master, moment_one, moment_two):
    num_experts = lax.axis_size("expert")
    recv_rows = hidden.shape[2]
    capacity = recv_rows // num_experts
    features = cotangent.shape[1]
    expert_ids = jnp.arange(num_experts, dtype=jnp.int32)
    route_flat = route[:, 0]
    one_hot = (route_flat[:, None] == expert_ids[None, :]).astype(jnp.int32)
    rank = jnp.sum((jnp.cumsum(one_hot, axis=0) - one_hot) * one_hot, axis=1)
    dest_row = route_flat * capacity + rank
    packed = jnp.zeros((num_experts * capacity, features), jnp.bfloat16).at[dest_row].set(cotangent)
    packed = packed.reshape(num_experts, capacity, features)
    received = lax.all_to_all(packed, "expert", split_axis=0, concat_axis=0, tiled=True).reshape(
        recv_rows, features
    )
    hidden_rows = hidden[0, 0]
    contract = (((0,), (0,)), ((), ()))
    grad_share = lax.psum_scatter(
        lax.dot_general(hidden_rows, received, contract, preferred_element_type=jnp.float32),
        "dp",
        scatter_dimension=0,
        tiled=True,
    )
    grad_share = grad_share.reshape(master.shape)
    moment_one_next = 0.9 * moment_one + 0.1 * grad_share
    moment_two_next = 0.95 * moment_two + 0.05 * grad_share * grad_share
    step_dir = (
        moment_one_next
        / (1.0 - 0.9**STEP)
        / (jnp.sqrt(moment_two_next / (1.0 - 0.95**STEP)) + 1e-08)
    )
    master_next = master - 0.01 * (step_dir + 0.1 * master)
    weights = lax.all_gather(master_next.astype(jnp.bfloat16), "dp", axis=1, tiled=True)
    return (master_next, moment_one_next, moment_two_next, weights)


def solution(mesh):
    return jax.shard_map(
        local,
        mesh=mesh,
        in_specs=(
            P(("dp", "expert"), None),
            P(("dp", "expert"), None),
            P("dp", "expert", None, None),
            P("expert", "dp", None),
            P("expert", "dp", None),
            P("expert", "dp", None),
        ),
        out_specs=(
            P("expert", "dp", None),
            P("expert", "dp", None),
            P("expert", "dp", None),
            P("expert", None, None),
        ),
        check_vma=False,
    )
```

profile of v0, /device:TPU:1, one launch (start us, length us, event | category | flops | bytes accessed | tf_op | source)
XLA Modules:
  0.0 255.9 jit_solution(6716429192361996441)
XLA Ops:
  7.2 0.0 copy-start
  7.2 0.0 reduce-scatter.4.cloned.1.call-start
  7.2 0.8 reduce
  8.1 0.9 reduce-window.6
  8.9 0.2 slice_reduce_fusion
  9.2 0.1 fusion.7
  9.3 0.7 fusion.9
  10.0 4.4 %scatter_custom_fusion = bf16[1152,1024]{1,0:T(8,128)(2,1)} fusion(s32[384]{0:T(512)S(1)} %fusion.9, bf16[384,1024]{1,0:T(8,128)(2,1)} %param.6, bf16[]{:T(256)} %constant.13.clone.1), kind=kCustom, calls=%fused_computation.3 | custom fusion | bytes 2359808 | tf_op jit(solution)/shard_map/scatter | solution.py:19
  14.4 35.2 %all_to_all.5 = bf16[16,72,1024]{2,1,0:T(8,128)(2,1)S(1)} all-to-all(bf16[16,72,1024]{2,1,0:T(8,128)(2,1)} %bitcast.39), channel_id=1, replica_groups=mesh['dp'=32,'expert'=16] {'expert'}, dimensions={0} | all-to-all | bytes 4718592 | tf_op jit(solution)/shard_map/all_to_all | solution.py:21
  49.6 0.0 copy-done
  49.6 4.0 %convolution_bitcast_fusion = f32[768,1024]{0,1:T(8,128)} fusion(bf16[1152,1024]{1,0:T(8,128)(2,1)S(1)} %bitcast.40, bf16[1,1,1152,768]{3,2,1,0:T(8,128)(2,1)S(1)} %copy-done), kind=kOutput, calls=%fused_computation.1 | convolution fusion | flops 1811939328 | bytes 7274496 | tf_op jit(solution)/shard_map/dot_general | solution.py:27
  53.6 3.5 %copy.40 = f32[768,1024]{1,0:T(8,128)} copy(f32[768,1024]{0,1:T(8,128)} %convolution_bitcast_fusion) | data formatting | bytes 6291456
  57.2 0.0 copy-start.1
  57.2 0.0 copy-start.2
  57.2 0.0 copy-start.3
  57.2 0.0 reduce-scatter.4.cloned.1.call-update
  57.2 0.0 all-gather.2.cloned.1.call-start
  57.3 113.7 %reduce-scatter.4.cloned.1.call-done = f32[24,1024]{1,0:T(8,128)} async-done(((f32[768,1024]{1,0:T(8,128)}), f32[24,1024]{1,0:T(8,128)}) %reduce-scatter.4.cloned.1.call-update) | async-done | bytes 98320 | tf_op jit(solution)/shard_map/reduce_scatter | solution.py:26
  171.0 0.0 copy-done.1
  171.0 0.0 copy-done.2
  171.0 0.0 copy-done.3
  171.0 1.7 fusion.10
  172.6 0.0 all-gather.2.cloned.1.call-update
  172.6 73.7 %all-gather.2.cloned.1.call-done = bf16[1,768,1024]{2,1,0:T(8,128)(2,1)} async-done(((bf16[1,24,1024]{2,1,0:T(8,128)(2,1)}), bf16[1,768,1024]{2,1,0:T(8,128)(2,1)}) %all-gather.2.cloned.1.call-update) | async-done | bytes 1572880 | tf_op jit(solution)/shard_map/all_gather | solution.py:41
  246.4 2.7 %copy.45 = bf16[1,768,1024]{2,1,0:T(8,128)(2,1)} copy(bf16[1,768,1024]{2,1,0:T(8,128)(2,1)} %all-gather.2.cloned.1.call-done) | data formatting | bytes 3145728
  (2 shorter events, 0.0 us)
Async XLA Ops:
  7.2 42.4 %copy-start = (bf16[1,1,1152,768]{3,2,1,0:T(8,128)(2,1)S(1)}, bf16[1,1,1152,768]{3,2,1,0:T(8,128)(2,1)}, u32[]{:S(2)}) copy-start(bf16[1,1,1152,768]{3,2,1,0:T(8,128)(2,1)} %param.8) | copy-start | bytes 5308420
  7.2 163.8 %reduce-scatter.4.cloned.1.call-start = ((), (), s32[]{:S(2)}) async-start(), calls=%async_computation.3 | async-start | bytes 3244032 | tf_op jit(solution)/shard_map/reduce_scatter | solution.py:26
  57.2 113.8 %copy-start.1 = (f32[1,24,1024]{2,1,0:T(8,128)S(1)}, f32[1,24,1024]{2,1,0:T(8,128)}, u32[]{:S(2)}) copy-start(f32[1,24,1024]{2,1,0:T(8,128)} %param.9) | copy-start | bytes 294916
  57.2 113.8 %copy-start.2 = (f32[1,24,1024]{2,1,0:T(8,128)S(1)}, f32[1,24,1024]{2,1,0:T(8,128)}, u32[]{:S(2)}) copy-start(f32[1,24,1024]{2,1,0:T(8,128)} %param.10) | copy-start | bytes 294916
  57.2 113.8 %copy-start.3 = (f32[1,24,1024]{2,1,0:T(8,128)S(1)}, f32[1,24,1024]{2,1,0:T(8,128)}, u32[]{:S(2)}) copy-start(f32[1,24,1024]{2,1,0:T(8,128)} %param.11) | copy-start | bytes 294916
  57.2 189.2 %all-gather.2.cloned.1.call-start = ((), (), s32[]{:S(2)}) async-start(), calls=%async_computation.2 | async-start | bytes 1622016 | tf_op jit(solution)/shard_map/all_gather | solution.py:41
Sparse Core Ops, SparseCore 0:
  57.3 113.5 reduce-scatter.3
  173.9 72.4 all-gather.1
where the time goes:
time: 256 us
  waiting for transfers between devices  187 us (73%)
  blocking collectives  35.2 us (14%)
  between operations  14.1 us (6%)
  local copies, waits for them, and re-layouts  10.9 us (4%)
  other arithmetic  4.19 us (2%)
  matrix products  4.02 us (2%)
    reduce_scatter x1, waiting for transfers between devices, local(): lax.psum_scatter(lax.dot_general(hidden_rows, received, contract, preferr...  114 us
    all_gather x1, waiting for transfers between devices, local(): lax.all_gather(master_next.astype(jnp.bfloat16), 'dp', axis=1, tiled=True)  73.7 us
    all_to_all x1, blocking collectives, local(): lax.all_to_all(packed, 'expert', split_axis=0, concat_axis=0, tiled=True)  35.2 us
    unnamed x10, local copies, waits for them, and re-layouts  6.23 us
  transfers between devices with their start and end apart: 2, of which 2 were waited for; matrix products, arithmetic and copies ran while one was open for 0% of the time, Pallas kernels for 0%

commit v1 on v0

v1 whole, which is shorter than its diff:
```python
import jax
import jax.numpy as jnp
from jax import lax
from jax.experimental import pallas as pl
from jax.experimental.pallas import tpu as pltpu
from jax.sharding import PartitionSpec as P

STEP = 10
FIXED = 65536.0
SMALL = 16.0
WEIGHT = 131072.0


def pack_kernel(capacity, route_ref, cot_ref, out_ref):
    tokens = cot_ref.shape[0]
    rows = out_ref.shape[0]
    block = 144
    col = route_ref[...]
    earlier = lax.broadcasted_iota(jnp.int32, (tokens, tokens), 0)
    token = lax.broadcasted_iota(jnp.int32, (tokens, tokens), 1)
    row = jnp.sum(jnp.where(earlier == token, col, 0), axis=0, keepdims=True)
    same = jnp.where((col == row) & (earlier < token), 1, 0)
    dest = row * capacity + jnp.sum(same, axis=0, keepdims=True)
    cot = cot_ref[...]
    for start in range(0, rows, block):
        slot = lax.broadcasted_iota(jnp.int32, (block, tokens), 0) + start
        pick = jnp.where(slot == dest, 1.0, 0.0).astype(jnp.bfloat16)
        out_ref[start : start + block, :] = jnp.dot(
            pick, cot, preferred_element_type=jnp.float32
        ).astype(jnp.bfloat16)


def pack(route, cotangent, num_experts, capacity):
    tokens, features = cotangent.shape
    rows = num_experts * capacity
    return pl.pallas_call(
        lambda *refs: pack_kernel(capacity, *refs),
        out_shape=jax.ShapeDtypeStruct((rows, features), jnp.bfloat16),
        in_specs=[pl.BlockSpec(memory_space=pltpu.VMEM)] * 2,
        out_specs=pl.BlockSpec(memory_space=pltpu.VMEM),
        compiler_params=pltpu.CompilerParams(vmem_limit_bytes=32 * 1024 * 1024),
        cost_estimate=pl.CostEstimate(
            flops=2 * rows * tokens * features, bytes_accessed=2 * (rows + tokens) * features, transcendentals=0
        ),
    )(route, cotangent)


def local(cotangent, route, hidden, master, moment_one, moment_two):
    num_experts = lax.axis_size("expert")
    n_dp = lax.axis_size("dp")
    recv_rows = hidden.shape[2]
    capacity = recv_rows // num_experts
    features = cotangent.shape[1]
    ff = hidden.shape[3]
    share = ff // n_dp
    pairs = n_dp // 4
    dp = lax.axis_index("dp")
    core = dp % 2
    pair = dp // 4

    ring = [[4 * p + r for p in range(pairs)] for r in range(4)]
    sides = [[4 * p + c, 4 * p + 2 + c] for p in range(pairs) for c in range(2)]
    quads = [[4 * p + r for r in range(4)] for p in range(pairs)]

    state = jnp.concatenate([master, moment_one, moment_two], axis=0)
    states = lax.all_gather(state, "dp", axis=0, tiled=False, axis_index_groups=ring)

    packed = pack(route, cotangent, num_experts, capacity).reshape(num_experts, capacity, features)
    received = lax.all_to_all(packed, "expert", split_axis=0, concat_axis=0, tiled=True).reshape(
        recv_rows, features
    )
    grad = lax.dot_general(
        hidden[0, 0], received, (((0,), (0,)), ((), ())), preferred_element_type=jnp.float32
    ).reshape(pairs, 2, 2, share, features)

    def of_core(which):
        return lax.dynamic_index_in_dim(grad, which, axis=2, keepdims=False)

    theirs = (of_core(1 - core) * SMALL).astype(jnp.float16)
    swap = [(d, d ^ 1) for d in range(n_dp)]
    other = lax.ppermute(theirs, "dp", swap)
    summed = of_core(core) * SMALL + other.astype(jnp.float32)
    halves = lax.all_to_all(
        summed.astype(jnp.float16).transpose(1, 0, 2, 3), "dp", 0, 0, tiled=True, axis_index_groups=sides
    )
    quarter = halves[0].astype(jnp.float32) + halves[1].astype(jnp.float32)
    fixed = jnp.round(quarter * (FIXED / SMALL)).astype(jnp.int32).astype(jnp.uint32)
    total = lax.psum(fixed, "dp", axis_index_groups=ring)
    gradient = total.astype(jnp.int32).astype(jnp.float32) * (1.0 / FIXED)

    m_all, one_all, two_all = states[:, 0], states[:, 1], states[:, 2]
    one_next = 0.9 * one_all + 0.1 * gradient
    two_next = 0.95 * two_all + 0.05 * gradient * gradient
    step_dir = one_next / (1.0 - 0.9**STEP) / (jnp.sqrt(two_next / (1.0 - 0.95**STEP)) + 1e-08)
    master_next = m_all - 0.01 * (step_dir + 0.1 * m_all)

    def own(x):
        return lax.dynamic_index_in_dim(x, pair, axis=0, keepdims=True)

    coded = (lax.reduce_precision(master_next, 8, 7) * WEIGHT).astype(jnp.float16)
    gathered = lax.all_gather(coded, "dp", axis=0, tiled=False, axis_index_groups=quads)
    weights = (gathered.astype(jnp.float32) * (1.0 / WEIGHT)).astype(jnp.bfloat16)
    weights = weights.transpose(1, 0, 2, 3).reshape(1, ff, features)
    return (own(master_next), own(one_next), own(two_next), weights)


def solution(mesh):
    return jax.shard_map(
        local,
        mesh=mesh,
        in_specs=(
            P(("dp", "expert"), None),
            P(("dp", "expert"), None),
            P("dp", "expert", None, None),
            P("expert", "dp", None),
            P("expert", "dp", None),
            P("expert", "dp", None),
        ),
        out_specs=(
            P("expert", "dp", None),
            P("expert", "dp", None),
            P("expert", "dp", None),
            P("expert", None, None),
        ),
        check_vma=False,
    )
```

time: 256 us -> 179 us (0.70)
  waiting for transfers between devices: 187 us -> 58.1 us
  blocking collectives: 35.2 us -> 67.4 us
  starting transfers between devices: 0.08 us -> 19.6 us
  local copies, waits for them, and re-layouts: 10.9 us -> 6.57 us
    reduce_scatter x1 -> x0, waiting for transfers between devices: 114 us -> none  [local(): lax.psum_scatter(lax.dot_general(hidden_rows, received, contract, preferr...]
    all_gather x1, waiting for transfers between devices: 73.7 us -> 0.02 us  [local(): lax.all_gather(state, 'dp', axis=0, tiled=False, axis_index_groups=ring)]
    all_to_all x0 -> x2, waiting for transfers between devices: none -> 56.2 us  [the longest x1 29.3 us: local(): lax.all_to_all(summed.astype(jnp.float16).transpose(1, 0, 2, 3), 'dp', 0,...]
    psum x0 -> x1, blocking collectives: none -> 50.9 us  [local(): total = lax.psum(fixed, 'dp', axis_index_groups=ring)]
    all_to_all x1 -> x0, blocking collectives: 35.2 us -> none  [local(): lax.all_to_all(packed, 'expert', split_axis=0, concat_axis=0, tiled=True)]
    all_gather x0 -> x1, blocking collectives: none -> 16.5 us  [local(): lax.all_gather(coded, 'dp', axis=0, tiled=False, axis_index_groups=quads)]
    all_to_all x0 -> x2, starting transfers between devices: none -> 11.3 us  [the longest x1 7.76 us: local(): lax.all_to_all(packed, 'expert', split_axis=0, concat_axis=0, tiled=True)]
    ppermute x0 -> x1, starting transfers between devices: none -> 8.26 us  [local(): other = lax.ppermute(theirs, 'dp', swap)]
  transfers between devices with their start and end apart: 2 -> 4, of which waited for: 2 -> 3; matrix products, arithmetic and copies ran while one was open for 0% -> 4% of each run, Pallas kernels for 0% -> 0%
where the time goes in v1:
time: 179 us; the launch traced here: 176 us
  blocking collectives  67.4 us (38%)
  waiting for transfers between devices  58.1 us (32%)
  starting transfers between devices  19.6 us (11%)
  between operations  14.2 us (8%)
  local copies, waits for them, and re-layouts  6.57 us (4%)
  other arithmetic  5.03 us (3%)
  matrix products  3.96 us (2%)
    psum x1, blocking collectives, local(): total = lax.psum(fixed, 'dp', axis_index_groups=ring)  50.9 us
    all_to_all x1, waiting for transfers between devices, local(): lax.all_to_all(summed.astype(jnp.float16).transpose(1, 0, 2, 3), 'dp', 0,...  29.3 us
    all_to_all x1, waiting for transfers between devices, local(): lax.all_to_all(packed, 'expert', split_axis=0, concat_axis=0, tiled=True)  26.9 us
    all_gather x1, blocking collectives, local(): lax.all_gather(coded, 'dp', axis=0, tiled=False, axis_index_groups=quads)  16.5 us
    ppermute x1, starting transfers between devices, local(): other = lax.ppermute(theirs, 'dp', swap)  8.26 us
    all_to_all x1, starting transfers between devices, local(): lax.all_to_all(packed, 'expert', split_axis=0, concat_axis=0, tiled=True)  7.76 us
    dot_general x1, matrix products, local(): lax.dot_general(hidden[0, 0], received, (((0,), (0,)), ((), ())), preferr...  3.96 us
  transfers between devices with their start and end apart: 4, of which 3 were waited for; matrix products, arithmetic and copies ran while one was open for 4% of the time, Pallas kernels for 0%

profile of v1, /device:TPU:1, one launch (start us, length us, event | category | flops | bytes accessed | tf_op | source)
XLA Modules:
  0.0 176.4 jit_solution(6407392870034823459)
XLA Ops:
  7.2 0.0 copy-start
  7.2 0.9 copy.22.refs_0_
  8.1 0.0 copy-start.2
  8.1 1.1 copy-done.2
  9.3 1.5 shard_map.93
  10.8 1.4 copy-done.1
  12.3 7.8 %all-to-all-start = ((bf16[16,72,1024]{2,1,0:T(8,128)(2,1)}), bf16[16,72,1024]{2,1,0:T(8,128)(2,1)}, u32[]{:S(2)}, u32[]{:S(2)}) async-start(bf16[16,72,1024]{2,1,0:T(8,128)(2,1)} %bitcast.54), calls=%async_computation | async-start | bytes 4718592 | tf_op jit(solution)/shard_map/all_to_all | solution.py:69
  20.0 0.0 all-gather.5.cloned.1.call-start
  20.1 0.0 copy-done.3
  20.1 0.0 copy-done.4
  20.1 0.0 copy-done.5
  20.1 0.7 pad_maximum_fusion
  20.9 0.0 all-gather.5.cloned.1.call-update
  20.9 26.9 %all-to-all-done = bf16[16,72,1024]{2,1,0:T(8,128)(2,1)} async-done(((bf16[16,72,1024]{2,1,0:T(8,128)(2,1)}), bf16[16,72,1024]{2,1,0:T(8,128)(2,1)}, u32[]{:S(2)}, u32[]{:S(2)}) %all-to-all-start) | async-done | bytes 2359328 | tf_op jit(solution)/shard_map/all_to_all | solution.py:69
  47.8 0.0 copy-done
  47.8 4.0 %fusion = f32[1024,768]{0,1:T(8,128)S(1)} fusion(bf16[1152,1024]{1,0:T(8,128)(2,1)} %bitcast.4, bf16[1,1,1152,768]{3,2,1,0:T(8,128)(2,1)S(1)} %copy-done), kind=kOutput, calls=%fused_computation.1 | convolution fusion | flops 1811939328 | bytes 7274496 | tf_op jit(solution)/shard_map/dot_general | solution.py:72
  51.8 0.4 constant_dynamic-slice_fusion.4
  52.2 0.2 fusion.7
  52.4 8.3 %collective-permute-start = (f16[8,2,24,1024]{3,2,0,1:T(8,128)(2,1)S(1)}, f16[8,2,24,1024]{3,2,0,1:T(8,128)(2,1)S(1)}, u32[]{:S(2)}, u32[]{:S(2)}) collective-permute-start(f16[8,2,24,1024]{3,2,0,1:T(8,128)(2,1)S(1)} %fusion.7), channel_id=1, source_target_pairs={{0,16},{16,0},{32,48},{48,32},{64,80},{80,64},{96,112},{112,96},{1... | collective-permute-start | bytes 2359304 | tf_op jit(solution)/shard_map/ppermute | solution.py:81
  60.6 1.9 %collective-permute-done = f16[8,2,24,1024]{3,2,0,1:T(8,128)(2,1)S(1)} collective-permute-done((f16[8,2,24,1024]{3,2,0,1:T(8,128)(2,1)S(1)}, f16[8,2,24,1024]{3,2,0,1:T(8,128)(2,1)S(1)}, u32[]{:S(2)}, u32[]{:S(2)}) %collective-permute-start) | collective-permute-done | bytes 786464 | tf_op jit(solution)/shard_map/ppermute | solution.py:81
  62.5 1.2 fusion.6
  63.7 3.5 %all-to-all-start.1 = ((f16[2,8,24,1024]{3,2,1,0:T(8,128)(2,1)}), f16[2,8,24,1024]{3,2,1,0:T(8,128)(2,1)S(1)}, u32[]{:S(2)}, u32[]{:S(2)}) async-start(f16[2,8,24,1024]{3,2,1,0:T(8,128)(2,1)} %fusion.6), calls=%async_computation.1 | async-start | bytes 1572864 | tf_op jit(solution)/shard_map/all_to_all | solution.py:83
  67.3 29.3 %all-to-all-done.1 = f16[2,8,24,1024]{3,2,1,0:T(8,128)(2,1)S(1)} async-done(((f16[2,8,24,1024]{3,2,1,0:T(8,128)(2,1)}), f16[2,8,24,1024]{3,2,1,0:T(8,128)(2,1)S(1)}, u32[]{:S(2)}, u32[]{:S(2)}) %all-to-all-start.1) | async-done | bytes 786464 | tf_op jit(solution)/shard_map/all_to_all | solution.py:83
  96.5 0.1 convert_bitcast_fusion
  96.7 50.9 %all-reduce.1 = u32[8,24,1024]{2,1,0:T(8,128)S(1)} all-reduce(u32[8,24,1024]{2,1,0:T(8,128)S(1)} %convert_bitcast_fusion), channel_id=1, replica_groups={{0,64,128,192,256,320,384,448},{16,80,144,208,272,336,400,464},{32,96,1..., use_global_device_ids=true, to_apply=%region_0.1 | all-reduce | flops 196608 | bytes 1572864 | tf_op jit(solution)/shard_map/psum | solution.py:88
  147.6 0.0 all-gather.5.cloned.1.call-done
  147.6 2.4 %multiply_convert_fusion.1 = (f16[8,24,1024]{2,1,0:T(8,128)(2,1)S(1)}, f32[8,24,1024]{2,1,0:T(8,128)S(1)}, f32[8,24,1024]{2,1,0:T(8,128)S(1)}, f32[8,24,1024]{2,1,0:T(8,128)S(1)}) fusion(f32[8,3,24,1024]{3,2,1,0:T(8,128)} %bitcast.57, u32[8,24,1024]{2,1,0:T(8,128)S(1)} %all-reduce.1), kind=kLoop, calls=%fused_computation.20 | loop fusion | flops 4128768 | bytes 5898240 | tf_op jit(solution)/shard_map/convert_element_type | solution.py:100
  150.0 16.5 %all-gather.6 = f16[32,24,1024]{2,1,0:T(8,128)(2,1)S(1)} all-gather(f16[8,24,1024]{2,1,0:T(8,128)(2,1)S(1)} %get-tuple-element.4), channel_id=3, replica_groups={{0,16,32,48},{64,80,96,112},{128,144,160,176},{192,208,224,240},{256,27..., dimensions={0}, use_global_device_ids=true | all-gather | bytes 1966080 | tf_op jit(solution)/shard_map/all_gather | solution.py:101
  166.4 0.4 multiply_convert_fusion
  166.9 1.3 copy.25
  168.2 0.6 constant_dynamic-slice_fusion.2
  168.8 0.7 constant_dynamic-slice_fusion
  (4 shorter events, 0.0 us)
Async XLA Ops:
  7.2 40.7 %copy-start = (bf16[1,1,1152,768]{3,2,1,0:T(8,128)(2,1)S(1)}, bf16[1,1,1152,768]{3,2,1,0:T(8,128)(2,1)}, u32[]{:S(2)}) copy-start(bf16[1,1,1152,768]{3,2,1,0:T(8,128)(2,1)} %param.8) | copy-start | bytes 5308420
  8.1 1.1 copy-start.2
  10.8 1.4 copy-start.1
  12.3 7.8 %copy-start.3 = (f32[1,24,1024]{2,1,0:T(8,128)S(1)}, f32[1,24,1024]{2,1,0:T(8,128)}, u32[]{:S(2)}) copy-start(f32[1,24,1024]{2,1,0:T(8,128)} %param.11) | copy-start | bytes 294916
  12.3 7.8 %copy-start.4 = (f32[1,24,1024]{2,1,0:T(8,128)S(1)}, f32[1,24,1024]{2,1,0:T(8,128)}, u32[]{:S(2)}) copy-start(f32[1,24,1024]{2,1,0:T(8,128)} %param.10) | copy-start | bytes 294916
  12.3 7.8 %copy-start.5 = (f32[1,24,1024]{2,1,0:T(8,128)S(1)}, f32[1,24,1024]{2,1,0:T(8,128)}, u32[]{:S(2)}) copy-start(f32[1,24,1024]{2,1,0:T(8,128)} %param.9) | copy-start | bytes 294916
  12.3 35.5 %all-to-all-start = ((bf16[16,72,1024]{2,1,0:T(8,128)(2,1)}), bf16[16,72,1024]{2,1,0:T(8,128)(2,1)}, u32[]{:S(2)}, u32[]{:S(2)}) async-start(bf16[16,72,1024]{2,1,0:T(8,128)(2,1)} %bitcast.54), calls=%async_computation | async-start | bytes 4718592 | tf_op jit(solution)/shard_map/all_to_all | solution.py:69
  20.0 127.6 %all-gather.5.cloned.1.call-start = ((), (), s32[]{:S(2)}) async-start(), calls=%async_computation.2 | async-start | bytes 2654208 | tf_op jit(solution)/shard_map/all_gather | solution.py:66
  52.4 10.2 %collective-permute-start = (f16[8,2,24,1024]{3,2,0,1:T(8,128)(2,1)S(1)}, f16[8,2,24,1024]{3,2,0,1:T(8,128)(2,1)S(1)}, u32[]{:S(2)}, u32[]{:S(2)}) collective-permute-start(f16[8,2,24,1024]{3,2,0,1:T(8,128)(2,1)S(1)} %fusion.7), channel_id=1, source_target_pairs={{0,16},{16,0},{32,48},{48,32},{64,80},{80,64},{96,112},{112,96},{1... | collective-permute-start | bytes 2359304 | tf_op jit(solution)/shard_map/ppermute | solution.py:81
  63.7 32.8 %all-to-all-start.1 = ((f16[2,8,24,1024]{3,2,1,0:T(8,128)(2,1)}), f16[2,8,24,1024]{3,2,1,0:T(8,128)(2,1)S(1)}, u32[]{:S(2)}, u32[]{:S(2)}) async-start(f16[2,8,24,1024]{3,2,1,0:T(8,128)(2,1)} %fusion.6), calls=%async_computation.1 | async-start | bytes 1572864 | tf_op jit(solution)/shard_map/all_to_all | solution.py:83
Sparse Core Ops, SparseCore 0:
  23.0 79.4 all-gather.4

commit v2 on v1

v2 whole, which is shorter than its diff:
```python
import jax
import jax.numpy as jnp
from jax import lax
from jax.experimental import pallas as pl
from jax.experimental.pallas import tpu as pltpu
from jax.sharding import PartitionSpec as P

STEP = 10
SMALL = 16.0
WEIGHT = 131072.0


def pack_kernel(capacity, route_hbm, cot_hbm, out_hbm, route, cot, rows, route_sem, cot_sem, out_sems):
    tokens = cot.shape[0]
    block = 2 * capacity
    fetch_route = pltpu.make_async_copy(route_hbm, route, route_sem)
    fetch_cot = pltpu.make_async_copy(cot_hbm, cot, cot_sem)
    fetch_route.start()
    fetch_cot.start()
    fetch_route.wait()
    row = route[...]
    later = lax.broadcasted_iota(jnp.int32, (tokens, tokens), 1)
    token = lax.broadcasted_iota(jnp.int32, (tokens, tokens), 0)
    col = jnp.sum(jnp.where(later == token, row, 0), axis=1, keepdims=True)
    same = jnp.where((col == row) & (token < later), 1, 0)
    dest = row * capacity + jnp.sum(same, axis=0, keepdims=True)
    fetch_cot.wait()
    copies = []
    for part in range(rows.shape[0] // block):
        where = pl.ds(part * block, block)
        slot = lax.broadcasted_iota(jnp.int32, (block, tokens), 0) + part * block
        pick = jnp.where(slot == dest, 1.0, 0.0).astype(jnp.bfloat16)
        rows[where, :] = jnp.dot(pick, cot[...], preferred_element_type=jnp.float32).astype(jnp.bfloat16)
        copies.append(pltpu.make_async_copy(rows.at[where, :], out_hbm.at[where, :], out_sems.at[part]))
        copies[-1].start()
    for copy in copies:
        copy.wait()


def pack(route, cotangent, num_experts, capacity):
    tokens, features = cotangent.shape
    rows = num_experts * capacity
    return pl.pallas_call(
        lambda *refs: pack_kernel(capacity, *refs),
        out_shape=jax.ShapeDtypeStruct((rows, features), jnp.bfloat16),
        in_specs=[pl.BlockSpec(memory_space=pltpu.HBM)] * 2,
        out_specs=pl.BlockSpec(memory_space=pltpu.HBM),
        scratch_shapes=[
            pltpu.VMEM((1, tokens), jnp.int32),
            pltpu.VMEM((tokens, features), jnp.bfloat16),
            pltpu.VMEM((rows, features), jnp.bfloat16),
            pltpu.SemaphoreType.DMA,
            pltpu.SemaphoreType.DMA,
            pltpu.SemaphoreType.DMA((num_experts // 2,)),
        ],
        compiler_params=pltpu.CompilerParams(vmem_limit_bytes=60 * 1024 * 1024),
        cost_estimate=pl.CostEstimate(
            flops=2 * rows * tokens * features, bytes_accessed=2 * (rows + tokens) * features, transcendentals=0
        ),
    )(route.reshape(1, tokens), cotangent)


def product_kernel(units_ref, tokens_ref, out_ref):
    out_ref[...] = jnp.dot(units_ref[...], tokens_ref[...], preferred_element_type=jnp.float32) * SMALL


def product(units, tokens):
    rows, depth = units.shape
    features = tokens.shape[1]
    width = 512
    return pl.pallas_call(
        product_kernel,
        grid=(features // width,),
        out_shape=jax.ShapeDtypeStruct((rows, features), jnp.float32),
        in_specs=[pl.BlockSpec((rows, depth), lambda i: (0, 0)), pl.BlockSpec((depth, width), lambda i: (0, i))],
        out_specs=pl.BlockSpec((rows, width), lambda i: (0, i)),
        compiler_params=pltpu.CompilerParams(vmem_limit_bytes=16 * 1024 * 1024),
        cost_estimate=pl.CostEstimate(
            flops=2 * rows * depth * features,
            bytes_accessed=2 * depth * (rows + features) + 4 * rows * features,
            transcendentals=0,
        ),
    )(units, tokens)


def local(cotangent, route, hidden, master, moment_one, moment_two):
    num_experts = lax.axis_size("expert")
    n_dp = lax.axis_size("dp")
    recv_rows = hidden.shape[2]
    capacity = recv_rows // num_experts
    features = cotangent.shape[1]
    ff = hidden.shape[3]
    share = ff // n_dp
    chips = n_dp // 2
    pairs = n_dp // 4
    core = lax.axis_index("dp") % 2

    ring = [[4 * p + r for p in range(pairs)] for r in range(4)]
    sides = [[4 * p + c, 4 * p + 2 + c] for p in range(pairs) for c in range(2)]

    packed = pack(route, cotangent, num_experts, capacity).reshape(num_experts, capacity, features)
    received = lax.all_to_all(packed, "expert", split_axis=0, concat_axis=0, tiled=True).reshape(
        recv_rows, features
    )

    units = hidden[0, 0].T.reshape(chips, 2, share, recv_rows)

    def of_core(which):
        return lax.dynamic_index_in_dim(units, which, axis=1, keepdims=False).reshape(chips * share, recv_rows)

    units_mine, units_theirs = lax.optimization_barrier((of_core(core), of_core(1 - core)))
    theirs = product(units_theirs, received)
    other = lax.ppermute(theirs.astype(jnp.float16), "dp", [(d, d ^ 1) for d in range(n_dp)])
    mine = product(units_mine, received)
    summed = (mine + other.astype(jnp.float32)).astype(jnp.float16)
    summed = summed.reshape(pairs, 2, share, features).transpose(1, 0, 2, 3)
    halves = lax.all_to_all(summed, "dp", 0, 0, tiled=True, axis_index_groups=sides)
    quarter = (halves[0].astype(jnp.float32) + halves[1].astype(jnp.float32)).astype(jnp.float16)
    eighths = lax.all_to_all(quarter, "dp", 0, 0, tiled=True, axis_index_groups=ring)
    gradient = jnp.sum(eighths.astype(jnp.float32), axis=0, keepdims=True) * (1.0 / SMALL)

    one_next = 0.9 * moment_one + 0.1 * gradient
    two_next = 0.95 * moment_two + 0.05 * gradient * gradient
    step_dir = one_next / (1.0 - 0.9**STEP) / (jnp.sqrt(two_next / (1.0 - 0.95**STEP)) + 1e-08)
    master_next = master - 0.01 * (step_dir + 0.1 * master)
    coded = (lax.reduce_precision(master_next, 8, 7) * WEIGHT).astype(jnp.float16)
    gathered = lax.all_gather(coded, "dp", axis=1, tiled=True)
    weights = (gathered.astype(jnp.float32) * (1.0 / WEIGHT)).astype(jnp.bfloat16)
    return (master_next, one_next, two_next, weights)


def solution(mesh):
    return jax.shard_map(
        local,
        mesh=mesh,
        in_specs=(
            P(("dp", "expert"), None),
            P(("dp", "expert"), None),
            P("dp", "expert", None, None),
            P("expert", "dp", None),
            P("expert", "dp", None),
            P("expert", "dp", None),
        ),
        out_specs=(
            P("expert", "dp", None),
            P("expert", "dp", None),
            P("expert", "dp", None),
            P("expert", None, None),
        ),
        check_vma=False,
    )
```

time: 179 us -> 143 us (0.80); the launches traced: 176 us -> 143 us
  waiting for transfers between devices: 58.1 us -> 21.6 us
  blocking collectives: 67.4 us -> 87.6 us
  between operations: 14.2 us -> 0.75 us
  Pallas kernels: 1.54 us -> 6.62 us
  starting transfers between devices: 19.6 us -> 15.5 us
  matrix products: 3.96 us -> 0 us
  other arithmetic: 5.03 us -> 2.9 us
    psum x1 -> x0, blocking collectives: 50.9 us -> none  [local(): total = lax.psum(fixed, 'dp', axis_index_groups=ring)]
    all_to_all x0 -> x2, blocking collectives: none -> 50.8 us  [the longest x1 36.9 us: local(): lax.all_to_all(quarter, 'dp', 0, 0, tiled=True, axis_index_groups=ring)]
    all_to_all x1 -> x0, waiting for transfers between devices: 29.3 us -> none  [local(): lax.all_to_all(summed.astype(jnp.float16).transpose(1, 0, 2, 3), 'dp', 0,...]
    all_gather x1, blocking collectives: 16.5 us -> 36.8 us  [local(): gathered = lax.all_gather(coded, 'dp', axis=1, tiled=True)]
    all_to_all x1, waiting for transfers between devices: 26.9 us -> 21.3 us  [local(): lax.all_to_all(packed, 'expert', split_axis=0, concat_axis=0, tiled=True)]
    dot_general x1 -> x0, matrix products: 3.96 us -> none  [local(): lax.dot_general(hidden[0, 0], received, (((0,), (0,)), ((), ())), preferr...]
    all_to_all x1 -> x0, starting transfers between devices: 3.54 us -> none  [local(): lax.all_to_all(summed.astype(jnp.float16).transpose(1, 0, 2, 3), 'dp', 0,...]
    pallas_call x0 -> x2, Pallas kernels: none -> 3.29 us  [product(): pl.pallas_call(product_kernel, grid=(features // width,), out_shape=jax.S...]
  transfers between devices with their start and end apart: 4 -> 2, of which waited for: 3 -> 2; matrix products, arithmetic and copies ran while one was open for 4% -> 4% of each run, Pallas kernels for 0% -> 1%
where the time goes in v2:
time: 143 us
  blocking collectives  87.6 us (61%)
  waiting for transfers between devices  21.6 us (15%)
  starting transfers between devices  15.5 us (11%)
  local copies, waits for them, and re-layouts  7.66 us (5%)
  Pallas kernels  6.62 us (5%)
  other arithmetic  2.9 us (2%)
    all_to_all x1, blocking collectives, local(): lax.all_to_all(quarter, 'dp', 0, 0, tiled=True, axis_index_groups=ring)  36.9 us
    all_gather x1, blocking collectives, local(): gathered = lax.all_gather(coded, 'dp', axis=1, tiled=True)  36.8 us
    all_to_all x1, waiting for transfers between devices, local(): lax.all_to_all(packed, 'expert', split_axis=0, concat_axis=0, tiled=True)  21.3 us
    all_to_all x1, blocking collectives, local(): lax.all_to_all(summed, 'dp', 0, 0, tiled=True, axis_index_groups=sides)  13.9 us
    ppermute x1, starting transfers between devices, local(): lax.ppermute(theirs.astype(jnp.float16), 'dp', [(d, d ^ 1) for d in range...  7.88 us
    all_to_all x1, starting transfers between devices, local(): lax.all_to_all(packed, 'expert', split_axis=0, concat_axis=0, tiled=True)  7.59 us
    unnamed x9, local copies, waits for them, and re-layouts  5.04 us
    pallas_call x1, Pallas kernels, pack(): pl.pallas_call(lambda *refs: pack_kernel(capacity, *refs), out_shape=jax....  3.34 us
  transfers between devices with their start and end apart: 2, of which 2 were waited for; matrix products, arithmetic and copies ran while one was open for 4% of the time, Pallas kernels for 1%

profile of v2, /device:TPU:1, one launch (start us, length us, event | category | flops | bytes accessed | tf_op | source)
XLA Modules:
  0.0 142.6 jit_solution(16229446978633782840)
XLA Ops:
  0.6 3.3 %shard_map.93 = bf16[1152,1024]{1,0:T(8,128)(2,1)} custom-call(s32[1,384]{1,0:T(1,128)} %bitcast.30, bf16[384,1024]{1,0:T(8,128)(2,1)} %refs_1_.1), custom_call_target="tpu_custom_call" | custom-call | flops 905969664 | bytes 3145728 | tf_op jit(solution)/shard_map/pallas_call | solution.py:43
  4.0 7.6 %all-to-all-start = ((bf16[16,72,1024]{2,1,0:T(8,128)(2,1)}), bf16[16,72,1024]{2,1,0:T(8,128)(2,1)S(1)}, u32[]{:S(2)}, u32[]{:S(2)}) async-start(bf16[16,72,1024]{2,1,0:T(8,128)(2,1)} %bitcast.29), calls=%async_computation | async-start | bytes 4718592 | tf_op jit(solution)/shard_map/all_to_all | solution.py:102
  11.6 3.9 %copy.13 = bf16[1,1,1152,768]{2,3,1,0:T(8,128)(2,1)} copy(bf16[1,1,1152,768]{3,2,1,0:T(8,128)(2,1)} %param.8) | data formatting | bytes 3538944 | tf_op args[2]
  15.5 2.5 %constant_dynamic-slice_fusion = (bf16[16,1,24,1152]{3,2,1,0:T(8,128)(2,1)}, bf16[16,1,24,1152]{3,2,1,0:T(8,128)(2,1)S(1)}) fusion(bf16[16,2,24,1152]{3,2,1,0:T(8,128)(2,1)} %bitcast.26, s32[]{:T(128)S(6)} %select_n.16, s32[]{:T(128)S(6)} %select_n.15), kind=kLoop, calls=%fused_computation.10 | loop fusion | bytes 3538952 | tf_op jit(solution)/shard_map/jit(dynamic_index_in_dim)/dynamic_slice | solution.py:109
  17.9 21.3 %all-to-all-done = bf16[16,72,1024]{2,1,0:T(8,128)(2,1)S(1)} async-done(((bf16[16,72,1024]{2,1,0:T(8,128)(2,1)}), bf16[16,72,1024]{2,1,0:T(8,128)(2,1)S(1)}, u32[]{:S(2)}, u32[]{:S(2)}) %all-to-all-start) | async-done | bytes 2359328 | tf_op jit(solution)/shard_map/all_to_all | solution.py:102
  39.3 0.0 copy-start
  39.3 1.2 copy-done
  40.4 1.6 %shard_map.95 = f32[384,1024]{1,0:T(8,128)S(1)} custom-call(bf16[384,1152]{1,0:T(8,128)(2,1)S(1)} %bitcast.25, bf16[1152,1024]{1,0:T(8,128)(2,1)S(1)} %bitcast.22), custom_call_target="tpu_custom_call" | custom-call | flops 905969664 | bytes 4816896 | tf_op jit(solution)/shard_map/pallas_call | solution.py:71
  42.1 0.1 convert_element_type.35
  42.2 7.9 %collective-permute-start = (f16[384,1024]{1,0:T(8,128)(2,1)S(1)}, f16[384,1024]{1,0:T(8,128)(2,1)S(1)}, u32[]{:S(2)}, u32[]{:S(2)}) collective-permute-start(f16[384,1024]{1,0:T(8,128)(2,1)S(1)} %convert_element_type.35), channel_id=1, source_target_pairs={{0,16},{16,0},{32,48},{48,32},{64,80},{80,64},{96,112},{112,96},{1... | collective-permute-start | bytes 2359304 | tf_op jit(solution)/shard_map/ppermute | solution.py:113
  50.1 1.6 %shard_map.94 = f32[384,1024]{1,0:T(8,128)S(1)} custom-call(bf16[384,1152]{1,0:T(8,128)(2,1)S(1)} %bitcast.24, bf16[1152,1024]{1,0:T(8,128)(2,1)S(1)} %bitcast.23), custom_call_target="tpu_custom_call" | custom-call | flops 905969664 | bytes 4816896 | tf_op jit(solution)/shard_map/pallas_call | solution.py:71
  51.8 0.2 collective-permute-done
  52.0 0.3 add_convert_fusion
  52.3 0.1 copy.16
  52.4 13.9 %all_to_all.15 = f16[2,8,24,1024]{3,2,1,0:T(8,128)(2,1)S(1)} all-to-all(f16[2,8,24,1024]{3,2,1,0:T(8,128)(2,1)S(1)} %bitcast.27), channel_id=1, replica_groups={{0,32},{16,48},{64,96},{80,112},{128,160},{144,176},{192,224},{208,240}..., dimensions={0} | all-to-all | bytes 1572864 | tf_op jit(solution)/shard_map/all_to_all | solution.py:117
  66.3 0.0 copy-start.1
  66.3 0.0 copy-start.2
  66.3 0.0 copy-start.3
  66.3 0.1 fusion
  66.4 36.9 %all_to_all.16 = f16[8,24,1024]{2,1,0:T(8,128)(2,1)S(1)} all-to-all(f16[8,24,1024]{2,1,0:T(8,128)(2,1)S(1)} %fusion), channel_id=1, replica_groups={{0,64,128,192,256,320,384,448},{16,80,144,208,272,336,400,464},{32,96,1..., dimensions={0} | all-to-all | bytes 786432 | tf_op jit(solution)/shard_map/all_to_all | solution.py:119
  103.3 0.1 convert_reduce_fusion
  103.4 0.0 copy-done.1
  103.4 0.0 copy-done.2
  103.4 0.0 copy-done.3
  103.4 0.8 multiply_convert_fusion.1
  104.2 36.8 %all-gather.1 = f16[1,768,1024]{2,1,0:T(8,128)(2,1)S(1)} all-gather(f16[1,24,1024]{2,1,0:T(8,128)(2,1)S(1)} %get-tuple-element.8), channel_id=1, replica_groups=mesh['dp'=32,'expert'=16] {'dp'}, dimensions={1}, use_global_device_ids=true | all-gather | bytes 1622016 | tf_op jit(solution)/shard_map/all_gather | solution.py:127
  141.0 1.6 %multiply_convert_fusion = bf16[1,768,1024]{2,1,0:T(8,128)(2,1)} fusion(f16[1,768,1024]{2,1,0:T(8,128)(2,1)S(1)} %all-gather.1), kind=kLoop, calls=%fused_computation | loop fusion | flops 2359296 | bytes 3145728 | tf_op jit(solution)/shard_map/convert_element_type | solution.py:128
Async XLA Ops:
  4.0 35.3 %all-to-all-start = ((bf16[16,72,1024]{2,1,0:T(8,128)(2,1)}), bf16[16,72,1024]{2,1,0:T(8,128)(2,1)S(1)}, u32[]{:S(2)}, u32[]{:S(2)}) async-start(bf16[16,72,1024]{2,1,0:T(8,128)(2,1)} %bitcast.29), calls=%async_computation | async-start | bytes 4718592 | tf_op jit(solution)/shard_map/all_to_all | solution.py:102
  39.3 1.2 copy-start
  42.2 9.8 %collective-permute-start = (f16[384,1024]{1,0:T(8,128)(2,1)S(1)}, f16[384,1024]{1,0:T(8,128)(2,1)S(1)}, u32[]{:S(2)}, u32[]{:S(2)}) collective-permute-start(f16[384,1024]{1,0:T(8,128)(2,1)S(1)} %convert_element_type.35), channel_id=1, source_target_pairs={{0,16},{16,0},{32,48},{48,32},{64,80},{80,64},{96,112},{112,96},{1... | collective-permute-start | bytes 2359304 | tf_op jit(solution)/shard_map/ppermute | solution.py:113
  66.3 37.1 %copy-start.1 = (f32[1,24,1024]{2,1,0:T(8,128)S(1)}, f32[1,24,1024]{2,1,0:T(8,128)}, u32[]{:S(2)}) copy-start(f32[1,24,1024]{2,1,0:T(8,128)} %param.9) | copy-start | bytes 294916
  66.3 37.1 %copy-start.2 = (f32[1,24,1024]{2,1,0:T(8,128)S(1)}, f32[1,24,1024]{2,1,0:T(8,128)}, u32[]{:S(2)}) copy-start(f32[1,24,1024]{2,1,0:T(8,128)} %param.10) | copy-start | bytes 294916
  66.3 37.1 %copy-start.3 = (f32[1,24,1024]{2,1,0:T(8,128)S(1)}, f32[1,24,1024]{2,1,0:T(8,128)}, u32[]{:S(2)}) copy-start(f32[1,24,1024]{2,1,0:T(8,128)} %param.11) | copy-start | bytes 294916

commit v3 on v2

--- a/solution.py
+++ b/solution.py
@@ -10,31 +10,21 @@
 WEIGHT = 131072.0
 
 
-def pack_kernel(capacity, route_hbm, cot_hbm, out_hbm, route, cot, rows, route_sem, cot_sem, out_sems):
-    tokens = cot.shape[0]
+def pack_kernel(capacity, route_ref, cot_ref, out_ref):
+    tokens = cot_ref.shape[0]
     block = 2 * capacity
-    fetch_route = pltpu.make_async_copy(route_hbm, route, route_sem)
-    fetch_cot = pltpu.make_async_copy(cot_hbm, cot, cot_sem)
-    fetch_route.start()
-    fetch_cot.start()
-    fetch_route.wait()
-    row = route[...]
+    row = route_ref[...]
     later = lax.broadcasted_iota(jnp.int32, (tokens, tokens), 1)
     token = lax.broadcasted_iota(jnp.int32, (tokens, tokens), 0)
     col = jnp.sum(jnp.where(later == token, row, 0), axis=1, keepdims=True)
     same = jnp.where((col == row) & (token < later), 1, 0)
     dest = row * capacity + jnp.sum(same, axis=0, keepdims=True)
-    fetch_cot.wait()
-    copies = []
-    for part in range(rows.shape[0] // block):
-        where = pl.ds(part * block, block)
-        slot = lax.broadcasted_iota(jnp.int32, (block, tokens), 0) + part * block
+    for start in range(0, out_ref.shape[0], block):
+        slot = lax.broadcasted_iota(jnp.int32, (block, tokens), 0) + start
         pick = jnp.where(slot == dest, 1.0, 0.0).astype(jnp.bfloat16)
-        rows[where, :] = jnp.dot(pick, cot[...], preferred_element_type=jnp.float32).astype(jnp.bfloat16)
-        copies.append(pltpu.make_async_copy(rows.at[where, :], out_hbm.at[where, :], out_sems.at[part]))
-        copies[-1].start()
-    for copy in copies:
-        copy.wait()
+        out_ref[start : start + block, :] = jnp.dot(
+            pick, cot_ref[...], preferred_element_type=jnp.float32
+        ).astype(jnp.bfloat16)
 
 
 def pack(route, cotangent, num_experts, capacity):
@@ -43,17 +33,9 @@
     return pl.pallas_call(
         lambda *refs: pack_kernel(capacity, *refs),
         out_shape=jax.ShapeDtypeStruct((rows, features), jnp.bfloat16),
-        in_specs=[pl.BlockSpec(memory_space=pltpu.HBM)] * 2,
-        out_specs=pl.BlockSpec(memory_space=pltpu.HBM),
-        scratch_shapes=[
-            pltpu.VMEM((1, tokens), jnp.int32),
-            pltpu.VMEM((tokens, features), jnp.bfloat16),
-            pltpu.VMEM((rows, features), jnp.bfloat16),
-            pltpu.SemaphoreType.DMA,
-            pltpu.SemaphoreType.DMA,
-            pltpu.SemaphoreType.DMA((num_experts // 2,)),
-        ],
-        compiler_params=pltpu.CompilerParams(vmem_limit_bytes=60 * 1024 * 1024),
+        in_specs=[pl.BlockSpec(memory_space=pltpu.VMEM)] * 2,
+        out_specs=pl.BlockSpec(memory_space=pltpu.VMEM),
+        compiler_params=pltpu.CompilerParams(vmem_limit_bytes=16 * 1024 * 1024),
         cost_estimate=pl.CostEstimate(
             flops=2 * rows * tokens * features, bytes_accessed=2 * (rows + tokens) * features, transcendentals=0
         ),
@@ -98,18 +80,19 @@
     ring = [[4 * p + r for p in range(pairs)] for r in range(4)]
     sides = [[4 * p + c, 4 * p + 2 + c] for p in range(pairs) for c in range(2)]
 
-    packed = pack(route, cotangent, num_experts, capacity).reshape(num_experts, capacity, features)
-    received = lax.all_to_all(packed, "expert", split_axis=0, concat_axis=0, tiled=True).reshape(
-        recv_rows, features
-    )
-
     units = hidden[0, 0].T.reshape(chips, 2, share, recv_rows)
 
     def of_core(which):
         return lax.dynamic_index_in_dim(units, which, axis=1, keepdims=False).reshape(chips * share, recv_rows)
 
-    units_mine, units_theirs = lax.optimization_barrier((of_core(core), of_core(1 - core)))
-    theirs = product(units_theirs, received)
+    packed = pack(route, cotangent, num_experts, capacity)
+    packed, units_mine, units_theirs = lax.optimization_barrier((packed, of_core(core), of_core(1 - core)))
+    packed = packed.reshape(num_experts, capacity, features)
+    received = lax.all_to_all(packed, "expert", split_axis=0, concat_axis=0, tiled=True).reshape(
+        recv_rows, features
+    )
+
+    theirs = jnp.dot(units_theirs, received, preferred_element_type=jnp.float32) * SMALL
     other = lax.ppermute(theirs.astype(jnp.float16), "dp", [(d, d ^ 1) for d in range(n_dp)])
     mine = product(units_mine, received)
     summed = (mine + other.astype(jnp.float32)).astype(jnp.float16)

time: 143 us -> 140 us (0.979)
  blocking collectives: 87.6 us -> 123 us
  waiting for transfers between devices: 21.6 us -> 0.23 us
  starting transfers between devices: 15.5 us -> 5.5 us
  local copies, waits for them, and re-layouts: 7.66 us -> 3.12 us
  Pallas kernels: 6.62 us -> 3.21 us
    all_to_all x0 -> x1, blocking collectives: none -> 35.8 us  [local(): lax.all_to_all(packed, 'expert', split_axis=0, concat_axis=0, tiled=True)]
    all_to_all x1 -> x0, waiting for transfers between devices: 21.3 us -> none  [local(): lax.all_to_all(packed, 'expert', split_axis=0, concat_axis=0, tiled=True)]
    all_to_all x1 -> x0, starting transfers between devices: 7.59 us -> none  [local(): lax.all_to_all(packed, 'expert', split_axis=0, concat_axis=0, tiled=True)]
    ppermute x1, starting transfers between devices: 7.88 us -> 5.5 us  [local(): lax.ppermute(theirs.astype(jnp.float16), 'dp', [(d, d ^ 1) for d in range...]
    dynamic_slice x1, local copies, waits for them, and re-layouts: 2.48 us -> 0.15 us  [of_core(): lax.dynamic_index_in_dim(units, which, axis=1, keepdims=False)]
    unnamed x9 -> x11, local copies, waits for them, and re-layouts: 5.04 us -> 2.83 us
    pallas_call x1, Pallas kernels: 3.34 us -> 1.56 us  [pack(): pl.pallas_call(lambda *refs: pack_kernel(capacity, *refs), out_shape=jax....]
    pallas_call x2 -> x1, Pallas kernels: 3.29 us -> 1.65 us  [product(): pl.pallas_call(product_kernel, grid=(features // width,), out_shape=jax.S...]
  transfers between devices with their start and end apart: 2 -> 1, of which waited for: 2 -> 1; matrix products, arithmetic and copies ran while one was open for 4% -> 0% of each run, Pallas kernels for 1% -> 1%
where the time goes in v3:
time: 140 us; the launch traced here: 139 us
  blocking collectives  123 us (88%)
  starting transfers between devices  5.5 us (4%)
  Pallas kernels  3.21 us (2%)
  local copies, waits for them, and re-layouts  3.12 us (2%)
  other arithmetic  2.8 us (2%)
    all_to_all x1, blocking collectives, local(): lax.all_to_all(quarter, 'dp', 0, 0, tiled=True, axis_index_groups=ring)  36.9 us
    all_gather x1, blocking collectives, local(): gathered = lax.all_gather(coded, 'dp', axis=1, tiled=True)  36.8 us
    all_to_all x1, blocking collectives, local(): lax.all_to_all(packed, 'expert', split_axis=0, concat_axis=0, tiled=True)  35.8 us
    all_to_all x1, blocking collectives, local(): lax.all_to_all(summed, 'dp', 0, 0, tiled=True, axis_index_groups=sides)  13.1 us
    ppermute x1, starting transfers between devices, local(): lax.ppermute(theirs.astype(jnp.float16), 'dp', [(d, d ^ 1) for d in range...  5.5 us
    unnamed x11, local copies, waits for them, and re-layouts  2.83 us
  transfers between devices with their start and end apart: 1, of which 1 were waited for; matrix products, arithmetic and copies ran while one was open for 0% of the time, Pallas kernels for 1%

profile of v3, /device:TPU:1, one launch (start us, length us, event | category | flops | bytes accessed | tf_op | source)
XLA Modules:
  0.0 139.4 jit_solution(16085413578779869344)
XLA Ops:
  0.6 0.0 copy-start
  0.7 0.0 copy-start.1
  0.7 2.8 %copy.12 = bf16[1,1,1152,768]{2,3,1,0:T(8,128)(2,1)S(1)} copy(bf16[1,1,1152,768]{3,2,1,0:T(8,128)(2,1)} %param.8) | data formatting | bytes 3538944 | tf_op args[2]
  3.5 0.0 copy-done
  3.5 0.0 copy-done.1
  3.5 1.6 %shard_map.93 = bf16[1152,1024]{1,0:T(8,128)(2,1)S(1)} custom-call(s32[1,384]{1,0:T(1,128)S(1)} %bitcast.28, bf16[384,1024]{1,0:T(8,128)(2,1)S(1)} %copy-done), custom_call_target="tpu_custom_call" | custom-call | flops 905969664 | bytes 3145728 | tf_op jit(solution)/shard_map/pallas_call | solution.py:33
  5.1 0.2 constant_dynamic-slice_fusion
  5.2 35.8 %all_to_all.15 = bf16[16,72,1024]{2,1,0:T(8,128)(2,1)S(1)} all-to-all(bf16[16,72,1024]{2,1,0:T(8,128)(2,1)S(1)} %bitcast.27), channel_id=1, replica_groups=mesh['dp'=32,'expert'=16] {'expert'}, dimensions={0} | all-to-all | bytes 4718592 | tf_op jit(solution)/shard_map/all_to_all | solution.py:91
  41.0 1.2 multiply_convert_fusion.1
  42.2 5.5 %collective-permute-start = (f16[384,1024]{1,0:T(8,128)(2,1)S(1)}, f16[384,1024]{1,0:T(8,128)(2,1)S(1)}, u32[]{:S(2)}, u32[]{:S(2)}) collective-permute-start(f16[384,1024]{1,0:T(8,128)(2,1)S(1)} %multiply_convert_fusion.1), channel_id=1, source_target_pairs={{0,16},{16,0},{32,48},{48,32},{64,80},{80,64},{96,112},{112,96},{1... | collective-permute-start | bytes 2359304 | tf_op jit(solution)/shard_map/ppermute | solution.py:96
  47.7 1.6 %shard_map.94 = f32[384,1024]{1,0:T(8,128)S(1)} custom-call(bf16[384,1152]{1,0:T(8,128)(2,1)S(1)} %bitcast.26, bf16[1152,1024]{1,0:T(8,128)(2,1)S(1)} %bitcast.25), custom_call_target="tpu_custom_call" | custom-call | flops 905969664 | bytes 4816896 | tf_op jit(solution)/shard_map/pallas_call | solution.py:53
  49.4 0.2 collective-permute-done
  49.6 0.3 add_convert_fusion
  49.9 0.1 copy.15
  50.0 0.0 copy-start.2
  50.0 0.0 copy-start.3
  50.0 0.0 copy-start.4
  50.0 13.1 %all_to_all.16 = f16[2,8,24,1024]{3,2,1,0:T(8,128)(2,1)S(1)} all-to-all(f16[2,8,24,1024]{3,2,1,0:T(8,128)(2,1)S(1)} %bitcast.30), channel_id=1, replica_groups={{0,32},{16,48},{64,96},{80,112},{128,160},{144,176},{192,224},{208,240}..., dimensions={0} | all-to-all | bytes 1572864 | tf_op jit(solution)/shard_map/all_to_all | solution.py:100
  63.1 0.1 fusion
  63.3 36.9 %all_to_all.17 = f16[8,24,1024]{2,1,0:T(8,128)(2,1)S(1)} all-to-all(f16[8,24,1024]{2,1,0:T(8,128)(2,1)S(1)} %fusion), channel_id=1, replica_groups={{0,64,128,192,256,320,384,448},{16,80,144,208,272,336,400,464},{32,96,1..., dimensions={0} | all-to-all | bytes 786432 | tf_op jit(solution)/shard_map/all_to_all | solution.py:102
  100.2 0.1 convert_reduce_fusion
  100.2 0.0 copy-done.2
  100.2 0.0 copy-done.3
  100.2 0.0 copy-done.4
  100.3 0.8 multiply_convert_fusion.2
  101.0 36.8 %all-gather.1 = f16[1,768,1024]{2,1,0:T(8,128)(2,1)S(1)} all-gather(f16[1,24,1024]{2,1,0:T(8,128)(2,1)S(1)} %get-tuple-element.10), channel_id=1, replica_groups=mesh['dp'=32,'expert'=16] {'dp'}, dimensions={1}, use_global_device_ids=true | all-gather | bytes 1622016 | tf_op jit(solution)/shard_map/all_gather | solution.py:110
  137.9 1.6 %multiply_convert_fusion = bf16[1,768,1024]{2,1,0:T(8,128)(2,1)} fusion(f16[1,768,1024]{2,1,0:T(8,128)(2,1)S(1)} %all-gather.1), kind=kLoop, calls=%fused_computation | loop fusion | flops 2359296 | bytes 3145728 | tf_op jit(solution)/shard_map/convert_element_type | solution.py:111
Async XLA Ops:
  0.6 2.8 %copy-start = (bf16[384,1024]{1,0:T(8,128)(2,1)S(1)}, bf16[384,1024]{1,0:T(8,128)(2,1)}, u32[]{:S(2)}) copy-start(bf16[384,1024]{1,0:T(8,128)(2,1)} %refs_1_.1) | copy-start | bytes 2359300
  0.7 2.8 %copy-start.1 = (s32[384,1]{0,1:T(1,128)S(1)}, s32[384,1]{0,1:T(1,128)}, u32[]{:S(2)}) copy-start(s32[384,1]{0,1:T(1,128)} %param.7) | copy-start | bytes 4612
  42.2 7.4 %collective-permute-start = (f16[384,1024]{1,0:T(8,128)(2,1)S(1)}, f16[384,1024]{1,0:T(8,128)(2,1)S(1)}, u32[]{:S(2)}, u32[]{:S(2)}) collective-permute-start(f16[384,1024]{1,0:T(8,128)(2,1)S(1)} %multiply_convert_fusion.1), channel_id=1, source_target_pairs={{0,16},{16,0},{32,48},{48,32},{64,80},{80,64},{96,112},{112,96},{1... | collective-permute-start | bytes 2359304 | tf_op jit(solution)/shard_map/ppermute | solution.py:96
  50.0 50.2 %copy-start.2 = (f32[1,24,1024]{2,1,0:T(8,128)S(1)}, f32[1,24,1024]{2,1,0:T(8,128)}, u32[]{:S(2)}) copy-start(f32[1,24,1024]{2,1,0:T(8,128)} %param.9) | copy-start | bytes 294916
  50.0 50.2 %copy-start.3 = (f32[1,24,1024]{2,1,0:T(8,128)S(1)}, f32[1,24,1024]{2,1,0:T(8,128)}, u32[]{:S(2)}) copy-start(f32[1,24,1024]{2,1,0:T(8,128)} %param.10) | copy-start | bytes 294916
  50.0 50.2 %copy-start.4 = (f32[1,24,1024]{2,1,0:T(8,128)S(1)}, f32[1,24,1024]{2,1,0:T(8,128)}, u32[]{:S(2)}) copy-start(f32[1,24,1024]{2,1,0:T(8,128)} %param.11) | copy-start | bytes 294916

commit v4 on v3

--- a/solution.py
+++ b/solution.py
@@ -10,7 +10,7 @@
 WEIGHT = 131072.0
 
 
-def pack_kernel(capacity, route_ref, cot_ref, out_ref):
+def pack_kernel(capacity, route_ref, cot_ref, hidden_ref, out_ref, units_ref):
     tokens = cot_ref.shape[0]
     block = 2 * capacity
     row = route_ref[...]
@@ -19,7 +19,10 @@
     col = jnp.sum(jnp.where(later == token, row, 0), axis=1, keepdims=True)
     same = jnp.where((col == row) & (token < later), 1, 0)
     dest = row * capacity + jnp.sum(same, axis=0, keepdims=True)
+    block = 128
     for start in range(0, out_ref.shape[0], block):
+        if start < hidden_ref.shape[0]:
+            units_ref[:, start : start + block] = hidden_ref[start : start + block, :].T
         slot = lax.broadcasted_iota(jnp.int32, (block, tokens), 0) + start
         pick = jnp.where(slot == dest, 1.0, 0.0).astype(jnp.bfloat16)
         out_ref[start : start + block, :] = jnp.dot(
@@ -27,19 +30,23 @@
         ).astype(jnp.bfloat16)
 
 
-def pack(route, cotangent, num_experts, capacity):
+def pack(route, cotangent, hidden, num_experts, capacity):
     tokens, features = cotangent.shape
+    depth, ff = hidden.shape
     rows = num_experts * capacity
     return pl.pallas_call(
         lambda *refs: pack_kernel(capacity, *refs),
-        out_shape=jax.ShapeDtypeStruct((rows, features), jnp.bfloat16),
-        in_specs=[pl.BlockSpec(memory_space=pltpu.VMEM)] * 2,
-        out_specs=pl.BlockSpec(memory_space=pltpu.VMEM),
+        out_shape=[
+            jax.ShapeDtypeStruct((rows, features), jnp.bfloat16),
+            jax.ShapeDtypeStruct((ff, depth), jnp.bfloat16),
+        ],
+        in_specs=[pl.BlockSpec(memory_space=pltpu.VMEM)] * 3,
+        out_specs=[pl.BlockSpec(memory_space=pltpu.VMEM)] * 2,
         compiler_params=pltpu.CompilerParams(vmem_limit_bytes=16 * 1024 * 1024),
         cost_estimate=pl.CostEstimate(
             flops=2 * rows * tokens * features, bytes_accessed=2 * (rows + tokens) * features, transcendentals=0
         ),
-    )(route.reshape(1, tokens), cotangent)
+    )(route.reshape(1, tokens), cotangent, hidden)
 
 
 def product_kernel(units_ref, tokens_ref, out_ref):
@@ -80,12 +87,14 @@
     ring = [[4 * p + r for p in range(pairs)] for r in range(4)]
     sides = [[4 * p + c, 4 * p + 2 + c] for p in range(pairs) for c in range(2)]
 
-    units = hidden[0, 0].T.reshape(chips, 2, share, recv_rows)
+    cut = 512
+    early = hidden[0, 0, :cut].T
+    packed, late = pack(route, cotangent, hidden[0, 0, cut:], num_experts, capacity)
+    units = jnp.concatenate([early, late], axis=1).reshape(chips, 2, share, recv_rows)
 
     def of_core(which):
         return lax.dynamic_index_in_dim(units, which, axis=1, keepdims=False).reshape(chips * share, recv_rows)
 
-    packed = pack(route, cotangent, num_experts, capacity)
     packed, units_mine, units_theirs = lax.optimization_barrier((packed, of_core(core), of_core(1 - core)))
     packed = packed.reshape(num_experts, capacity, features)
     received = lax.all_to_all(packed, "expert", split_axis=0, concat_axis=0, tiled=True).reshape(

time: 140 us -> 139 us (level)
    unnamed x11, local copies, waits for them, and re-layouts: 2.83 us -> 0.31 us
where the time goes in v4:
time: 139 us; the launch traced here: 138 us
  blocking collectives  123 us (88%)
  starting transfers between devices  5.51 us (4%)
  Pallas kernels  3.24 us (2%)
  other arithmetic  2.93 us (2%)
  local copies, waits for them, and re-layouts  1.99 us (1%)
    all_to_all x1, blocking collectives, local(): lax.all_to_all(quarter, 'dp', 0, 0, tiled=True, axis_index_groups=ring)  36.9 us
    all_gather x1, blocking collectives, local(): gathered = lax.all_gather(coded, 'dp', axis=1, tiled=True)  36.8 us
    all_to_all x1, blocking collectives, local(): lax.all_to_all(packed, 'expert', split_axis=0, concat_axis=0, tiled=True)  35.8 us
    all_to_all x1, blocking collectives, local(): lax.all_to_all(summed, 'dp', 0, 0, tiled=True, axis_index_groups=sides)  13.1 us
    ppermute x1, starting transfers between devices, local(): lax.ppermute(theirs.astype(jnp.float16), 'dp', [(d, d ^ 1) for d in range...  5.51 us
  transfers between devices with their start and end apart: 1, of which 1 were waited for; matrix products, arithmetic and copies ran while one was open for 0% of the time, Pallas kernels for 1%

profile of v4, /device:TPU:1, one launch (start us, length us, event | category | flops | bytes accessed | tf_op | source)
XLA Modules:
  0.0 138.5 jit_solution(11180636883023962661)
XLA Ops:
  0.6 0.0 slice-start
  0.7 0.0 copy-start
  0.7 0.0 copy-start.1
  0.7 1.4 slice_bitcast_fusion.refs_2_
  2.1 0.0 slice-done
  2.1 0.3 copy.15
  2.4 0.0 copy-done
  2.4 0.0 copy-done.1
  2.4 1.6 %shard_map.93 = (bf16[1152,1024]{1,0:T(8,128)(2,1)S(1)}, bf16[768,640]{1,0:T(8,128)(2,1)S(1)}) custom-call(s32[1,384]{1,0:T(1,128)S(1)} %bitcast.31, bf16[384,1024]{1,0:T(8,128)(2,1)S(1)} %copy-done, bf16[640,768]{1,0:T(8,128)(2,1)S(1)} %slice_bitcast_fusion.refs_2_), custom_call_target="tpu_custom_call" | custom-call | flops 905969664 | bytes 3145728 | tf_op jit(solution)/shard_map/pallas_call | solution.py:37
  4.0 0.1 pad_maximum_fusion
  4.1 0.2 constant_dynamic-slice_fusion
  4.3 35.8 %all_to_all.15 = bf16[16,72,1024]{2,1,0:T(8,128)(2,1)S(1)} all-to-all(bf16[16,72,1024]{2,1,0:T(8,128)(2,1)S(1)} %bitcast.30), channel_id=1, replica_groups=mesh['dp'=32,'expert'=16] {'expert'}, dimensions={0} | all-to-all | bytes 4718592 | tf_op jit(solution)/shard_map/all_to_all | solution.py:100
  40.1 1.2 multiply_convert_fusion.1
  41.2 5.5 %collective-permute-start = (f16[384,1024]{1,0:T(8,128)(2,1)S(1)}, f16[384,1024]{1,0:T(8,128)(2,1)S(1)}, u32[]{:S(2)}, u32[]{:S(2)}) collective-permute-start(f16[384,1024]{1,0:T(8,128)(2,1)S(1)} %multiply_convert_fusion.1), channel_id=1, source_target_pairs={{0,16},{16,0},{32,48},{48,32},{64,80},{80,64},{96,112},{112,96},{1... | collective-permute-start | bytes 2359304 | tf_op jit(solution)/shard_map/ppermute | solution.py:105
  46.8 1.7 %shard_map.94 = f32[384,1024]{1,0:T(8,128)S(1)} custom-call(bf16[384,1152]{1,0:T(8,128)(2,1)S(1)} %bitcast.29, bf16[1152,1024]{1,0:T(8,128)(2,1)S(1)} %bitcast.28), custom_call_target="tpu_custom_call" | custom-call | flops 905969664 | bytes 4816896 | tf_op jit(solution)/shard_map/pallas_call | solution.py:60
  48.4 0.2 collective-permute-done
  48.7 0.3 add_convert_fusion
  48.9 0.1 copy.18
  49.1 0.0 copy-start.2
  49.1 0.0 copy-start.3
  49.1 0.0 copy-start.4
  49.1 13.1 %all_to_all.16 = f16[2,8,24,1024]{3,2,1,0:T(8,128)(2,1)S(1)} all-to-all(f16[2,8,24,1024]{3,2,1,0:T(8,128)(2,1)S(1)} %bitcast.34), channel_id=1, replica_groups={{0,32},{16,48},{64,96},{80,112},{128,160},{144,176},{192,224},{208,240}..., dimensions={0} | all-to-all | bytes 1572864 | tf_op jit(solution)/shard_map/all_to_all | solution.py:109
  62.2 0.1 fusion
  62.3 36.9 %all_to_all.17 = f16[8,24,1024]{2,1,0:T(8,128)(2,1)S(1)} all-to-all(f16[8,24,1024]{2,1,0:T(8,128)(2,1)S(1)} %fusion), channel_id=1, replica_groups={{0,64,128,192,256,320,384,448},{16,80,144,208,272,336,400,464},{32,96,1..., dimensions={0} | all-to-all | bytes 786432 | tf_op jit(solution)/shard_map/all_to_all | solution.py:111
  99.2 0.1 convert_reduce_fusion
  99.3 0.0 copy-done.2
  99.3 0.0 copy-done.3
  99.3 0.0 copy-done.4
  99.3 0.8 multiply_convert_fusion.2
  100.1 36.8 %all-gather.1 = f16[1,768,1024]{2,1,0:T(8,128)(2,1)S(1)} all-gather(f16[1,24,1024]{2,1,0:T(8,128)(2,1)S(1)} %get-tuple-element.14), channel_id=1, replica_groups=mesh['dp'=32,'expert'=16] {'dp'}, dimensions={1}, use_global_device_ids=true | all-gather | bytes 1622016 | tf_op jit(solution)/shard_map/all_gather | solution.py:119
  136.9 1.6 %multiply_convert_fusion = bf16[1,768,1024]{2,1,0:T(8,128)(2,1)} fusion(f16[1,768,1024]{2,1,0:T(8,128)(2,1)S(1)} %all-gather.1), kind=kLoop, calls=%fused_computation | loop fusion | flops 2359296 | bytes 3145728 | tf_op jit(solution)/shard_map/convert_element_type | solution.py:120
Async XLA Ops:
  0.6 1.4 %slice-start = ((bf16[1,1,1152,768]{3,2,1,0:T(8,128)(2,1)}), bf16[1,1,512,768]{3,2,1,0:T(8,128)(2,1)S(1)}, s32[]{:S(2)}) async-start(bf16[1,1,1152,768]{3,2,1,0:T(8,128)(2,1)} %param.8), calls=%async_computation.3 | async-start | bytes 1572864 | tf_op jit(solution)/shard_map/slice | solution.py:91
  0.7 1.7 %copy-start = (bf16[384,1024]{1,0:T(8,128)(2,1)S(1)}, bf16[384,1024]{1,0:T(8,128)(2,1)}, u32[]{:S(2)}) copy-start(bf16[384,1024]{1,0:T(8,128)(2,1)} %refs_1_.1) | copy-start | bytes 2359300
  0.7 1.7 %copy-start.1 = (s32[384,1]{0,1:T(1,128)S(1)}, s32[384,1]{0,1:T(1,128)}, u32[]{:S(2)}) copy-start(s32[384,1]{0,1:T(1,128)} %param.7) | copy-start | bytes 4612
  41.2 7.4 %collective-permute-start = (f16[384,1024]{1,0:T(8,128)(2,1)S(1)}, f16[384,1024]{1,0:T(8,128)(2,1)S(1)}, u32[]{:S(2)}, u32[]{:S(2)}) collective-permute-start(f16[384,1024]{1,0:T(8,128)(2,1)S(1)} %multiply_convert_fusion.1), channel_id=1, source_target_pairs={{0,16},{16,0},{32,48},{48,32},{64,80},{80,64},{96,112},{112,96},{1... | collective-permute-start | bytes 2359304 | tf_op jit(solution)/shard_map/ppermute | solution.py:105
  49.1 50.2 %copy-start.2 = (f32[1,24,1024]{2,1,0:T(8,128)S(1)}, f32[1,24,1024]{2,1,0:T(8,128)}, u32[]{:S(2)}) copy-start(f32[1,24,1024]{2,1,0:T(8,128)} %param.9) | copy-start | bytes 294916
  49.1 50.2 %copy-start.3 = (f32[1,24,1024]{2,1,0:T(8,128)S(1)}, f32[1,24,1024]{2,1,0:T(8,128)}, u32[]{:S(2)}) copy-start(f32[1,24,1024]{2,1,0:T(8,128)} %param.10) | copy-start | bytes 294916
  49.1 50.2 %copy-start.4 = (f32[1,24,1024]{2,1,0:T(8,128)S(1)}, f32[1,24,1024]{2,1,0:T(8,128)}, u32[]{:S(2)}) copy-start(f32[1,24,1024]{2,1,0:T(8,128)} %param.11) | copy-start | bytes 294916

commit v5 on v4

--- a/solution.py
+++ b/solution.py
@@ -87,7 +87,7 @@
     ring = [[4 * p + r for p in range(pairs)] for r in range(4)]
     sides = [[4 * p + c, 4 * p + 2 + c] for p in range(pairs) for c in range(2)]
 
-    cut = 512
+    cut = 384
     early = hidden[0, 0, :cut].T
     packed, late = pack(route, cotangent, hidden[0, 0, cut:], num_experts, capacity)
     units = jnp.concatenate([early, late], axis=1).reshape(chips, 2, share, recv_rows)

time: 139 us -> 139 us (level)
  no operation moved by 1% of the time
where the time goes in v5:
time: 139 us
  blocking collectives  123 us (88%)
  starting transfers between devices  5.51 us (4%)
  Pallas kernels  3.24 us (2%)
  other arithmetic  2.95 us (2%)
  local copies, waits for them, and re-layouts  2.08 us (1%)
    all_to_all x1, blocking collectives, local(): lax.all_to_all(quarter, 'dp', 0, 0, tiled=True, axis_index_groups=ring)  36.9 us
    all_gather x1, blocking collectives, local(): gathered = lax.all_gather(coded, 'dp', axis=1, tiled=True)  36.8 us
    all_to_all x1, blocking collectives, local(): lax.all_to_all(packed, 'expert', split_axis=0, concat_axis=0, tiled=True)  35.8 us
    all_to_all x1, blocking collectives, local(): lax.all_to_all(summed, 'dp', 0, 0, tiled=True, axis_index_groups=sides)  13.1 us
    ppermute x1, starting transfers between devices, local(): lax.ppermute(theirs.astype(jnp.float16), 'dp', [(d, d ^ 1) for d in range...  5.51 us
  transfers between devices with their start and end apart: 1, of which 1 were waited for; matrix products, arithmetic and copies ran while one was open for 0% of the time, Pallas kernels for 1%

profile of v5, /device:TPU:1, one launch (start us, length us, event | category | flops | bytes accessed | tf_op | source)
XLA Modules:
  0.0 138.6 jit_solution(17837458792223842554)
XLA Ops:
  0.6 0.0 slice-start
  0.7 0.0 copy-start
  0.7 0.0 copy-start.1
  0.7 1.5 %slice_bitcast_fusion.refs_2_ = bf16[768,768]{1,0:T(8,128)(2,1)S(1)} fusion(bf16[1,1,1152,768]{3,2,1,0:T(8,128)(2,1)} %param.8), kind=kLoop, calls=%fused_computation.4 | loop fusion | bytes 2359296 | tf_op jit(solution)/shard_map/squeeze | solution.py:92
  2.1 0.0 slice-done
  2.1 0.3 copy.15
  2.5 0.0 copy-done
  2.5 0.0 copy-done.1
  2.5 1.6 %shard_map.93 = (bf16[1152,1024]{1,0:T(8,128)(2,1)S(1)}, bf16[768,768]{1,0:T(8,128)(2,1)S(1)}) custom-call(s32[1,384]{1,0:T(1,128)S(1)} %bitcast.31, bf16[384,1024]{1,0:T(8,128)(2,1)S(1)} %copy-done, bf16[768,768]{1,0:T(8,128)(2,1)S(1)} %slice_bitcast_fusion.refs_2_), custom_call_target="tpu_custom_call" | custom-call | flops 905969664 | bytes 3145728 | tf_op jit(solution)/shard_map/pallas_call | solution.py:37
  4.1 0.2 pad_maximum_fusion
  4.2 0.2 constant_dynamic-slice_fusion
  4.4 35.8 %all_to_all.15 = bf16[16,72,1024]{2,1,0:T(8,128)(2,1)S(1)} all-to-all(bf16[16,72,1024]{2,1,0:T(8,128)(2,1)S(1)} %bitcast.30), channel_id=1, replica_groups=mesh['dp'=32,'expert'=16] {'expert'}, dimensions={0} | all-to-all | bytes 4718592 | tf_op jit(solution)/shard_map/all_to_all | solution.py:100
  40.2 1.2 multiply_convert_fusion.1
  41.4 5.5 %collective-permute-start = (f16[384,1024]{1,0:T(8,128)(2,1)S(1)}, f16[384,1024]{1,0:T(8,128)(2,1)S(1)}, u32[]{:S(2)}, u32[]{:S(2)}) collective-permute-start(f16[384,1024]{1,0:T(8,128)(2,1)S(1)} %multiply_convert_fusion.1), channel_id=1, source_target_pairs={{0,16},{16,0},{32,48},{48,32},{64,80},{80,64},{96,112},{112,96},{1... | collective-permute-start | bytes 2359304 | tf_op jit(solution)/shard_map/ppermute | solution.py:105
  46.9 1.6 %shard_map.94 = f32[384,1024]{1,0:T(8,128)S(1)} custom-call(bf16[384,1152]{1,0:T(8,128)(2,1)S(1)} %bitcast.29, bf16[1152,1024]{1,0:T(8,128)(2,1)S(1)} %bitcast.28), custom_call_target="tpu_custom_call" | custom-call | flops 905969664 | bytes 4816896 | tf_op jit(solution)/shard_map/pallas_call | solution.py:60
  48.5 0.2 collective-permute-done
  48.8 0.3 add_convert_fusion
  49.0 0.1 copy.18
  49.2 0.0 copy-start.2
  49.2 0.0 copy-start.3
  49.2 0.0 copy-start.4
  49.2 13.1 %all_to_all.16 = f16[2,8,24,1024]{3,2,1,0:T(8,128)(2,1)S(1)} all-to-all(f16[2,8,24,1024]{3,2,1,0:T(8,128)(2,1)S(1)} %bitcast.33), channel_id=1, replica_groups={{0,32},{16,48},{64,96},{80,112},{128,160},{144,176},{192,224},{208,240}..., dimensions={0} | all-to-all | bytes 1572864 | tf_op jit(solution)/shard_map/all_to_all | solution.py:109
  62.3 0.1 fusion
  62.4 36.9 %all_to_all.17 = f16[8,24,1024]{2,1,0:T(8,128)(2,1)S(1)} all-to-all(f16[8,24,1024]{2,1,0:T(8,128)(2,1)S(1)} %fusion), channel_id=1, replica_groups={{0,64,128,192,256,320,384,448},{16,80,144,208,272,336,400,464},{32,96,1..., dimensions={0} | all-to-all | bytes 786432 | tf_op jit(solution)/shard_map/all_to_all | solution.py:111
  99.3 0.1 convert_reduce_fusion
  99.4 0.0 copy-done.2
  99.4 0.0 copy-done.3
  99.4 0.0 copy-done.4
  99.4 0.8 multiply_convert_fusion.2
  100.2 36.8 %all-gather.1 = f16[1,768,1024]{2,1,0:T(8,128)(2,1)S(1)} all-gather(f16[1,24,1024]{2,1,0:T(8,128)(2,1)S(1)} %get-tuple-element.14), channel_id=1, replica_groups=mesh['dp'=32,'expert'=16] {'dp'}, dimensions={1}, use_global_device_ids=true | all-gather | bytes 1622016 | tf_op jit(solution)/shard_map/all_gather | solution.py:119
  137.0 1.6 %multiply_convert_fusion = bf16[1,768,1024]{2,1,0:T(8,128)(2,1)} fusion(f16[1,768,1024]{2,1,0:T(8,128)(2,1)S(1)} %all-gather.1), kind=kLoop, calls=%fused_computation | loop fusion | flops 2359296 | bytes 3145728 | tf_op jit(solution)/shard_map/convert_element_type | solution.py:120
Async XLA Ops:
  0.6 1.5 %slice-start = ((bf16[1,1,1152,768]{3,2,1,0:T(8,128)(2,1)}), bf16[1,1,384,768]{3,2,1,0:T(8,128)(2,1)S(1)}, s32[]{:S(2)}) async-start(bf16[1,1,1152,768]{3,2,1,0:T(8,128)(2,1)} %param.8), calls=%async_computation.3 | async-start | bytes 1179648 | tf_op jit(solution)/shard_map/slice | solution.py:91
  0.7 1.8 %copy-start = (bf16[384,1024]{1,0:T(8,128)(2,1)S(1)}, bf16[384,1024]{1,0:T(8,128)(2,1)}, u32[]{:S(2)}) copy-start(bf16[384,1024]{1,0:T(8,128)(2,1)} %refs_1_.1) | copy-start | bytes 2359300
  0.7 1.8 %copy-start.1 = (s32[384,1]{0,1:T(1,128)S(1)}, s32[384,1]{0,1:T(1,128)}, u32[]{:S(2)}) copy-start(s32[384,1]{0,1:T(1,128)} %param.7) | copy-start | bytes 4612
  41.4 7.4 %collective-permute-start = (f16[384,1024]{1,0:T(8,128)(2,1)S(1)}, f16[384,1024]{1,0:T(8,128)(2,1)S(1)}, u32[]{:S(2)}, u32[]{:S(2)}) collective-permute-start(f16[384,1024]{1,0:T(8,128)(2,1)S(1)} %multiply_convert_fusion.1), channel_id=1, source_target_pairs={{0,16},{16,0},{32,48},{48,32},{64,80},{80,64},{96,112},{112,96},{1... | collective-permute-start | bytes 2359304 | tf_op jit(solution)/shard_map/ppermute | solution.py:105
  49.2 50.2 %copy-start.2 = (f32[1,24,1024]{2,1,0:T(8,128)S(1)}, f32[1,24,1024]{2,1,0:T(8,128)}, u32[]{:S(2)}) copy-start(f32[1,24,1024]{2,1,0:T(8,128)} %param.9) | copy-start | bytes 294916
  49.2 50.2 %copy-start.3 = (f32[1,24,1024]{2,1,0:T(8,128)S(1)}, f32[1,24,1024]{2,1,0:T(8,128)}, u32[]{:S(2)}) copy-start(f32[1,24,1024]{2,1,0:T(8,128)} %param.10) | copy-start | bytes 294916
  49.2 50.2 %copy-start.4 = (f32[1,24,1024]{2,1,0:T(8,128)S(1)}, f32[1,24,1024]{2,1,0:T(8,128)}, u32[]{:S(2)}) copy-start(f32[1,24,1024]{2,1,0:T(8,128)} %param.11) | copy-start | bytes 294916
